TPU v7x, 128 devices: a whole 4x4x4 slice. The times are simulated.
128 devices in a mesh: section: 8 (over x, y_hi), head: 8 (over z, y_lo), batch: 2 (over core).
Axes of the slice: x: 4, y: 4 (y_hi: 2, y_lo: 2; y = y_hi * 2 + y_lo), z: 4, core: 2. Of those that a mesh axis runs over, the one named last changes fastest.
Arguments:
- keys_prefill: bfloat16 [8, 32, 512, 1024], P('section', 'batch', None, 'head'), may hold values from -6 to 6
- values_prefill: bfloat16 [8, 32, 512, 1024], P('section', 'batch', None, 'head'), may hold values from -6 to 6
- lengths: int32 [32], replicated, may hold values from 1 to 510, 8192 in all
- slot_order: int32 [32], replicated, may hold values from 0 to 31, each once
- queries: bfloat16 [2, 8, 32, 8192], P(None, None, 'section'), may hold values from -51 to 51
- new_keys: bfloat16 [2, 8, 32, 1024], P(None, None, 'section'), may hold values from -5 to 5
- new_values: bfloat16 [2, 8, 32, 1024], P(None, None, 'section'), may hold values from -6 to 6
Outputs:
- attention: bfloat16 [2, 8, 32, 8192], P(None, None, 'section', ('head', 'batch'))
- keys_cache: bfloat16 [8, 32, 512, 1024], P(None, 'section', ('head', 'batch'))
- values_cache: bfloat16 [8, 32, 512, 1024], P(None, 'section', ('head', 'batch'))
Inputs may be any that keep to these rules, and one draw needn't show every extreme that they name: lengths[p] is the number of cached tokens of prompt p; the prefill cache holds stale values from position lengths[p] on, which are not part of the cache (zero in keys_cache and values_cache unless a new row is placed there, and never visible to attention). `slot_order`: each prompt appears in exactly one decode slot.
All inputs are finite; a program needn't handle non-finite values.
Results may differ from a plain program's by a relative error of at most 0.0044.
Values may be sent and summed in bfloat16 or wider, within the bound.
A program may use at most 128 MiB of HBM per device.

v0:
```python
import jax
import jax.numpy as jnp
from jax import lax
from jax.experimental import pallas as pl
from jax.experimental.pallas import tpu as pltpu
from jax.sharding import PartitionSpec as P

KVH = 8
HD = 128
GROUP = 8
BLOCK = 32
MESH = pl.DeviceIdType.MESH
HIDDEN = -1e30
BF16, F32 = jnp.bfloat16, jnp.float32


PLANE = {
    1: ((1, 1), (3, 3), (1, 3), (3, 1), (2, 1), (0, 3), (2, 3), (0, 1)),
    0: ((1, 0), (0, 2), (3, 2), (1, 2), (3, 0), (2, 2), (2, 0)),
}
def group_of(dx, low):
    return low * 4 + dx


def relay(
    slot_order_hbm, lengths_hbm, keys, values, keys_flat, values_flat, queries, new_keys, new_values,
    attention, values_cache, keys_land, keys_fresh, keep,
    key_columns, value_rows, keys_line, values_chip, keys_packed, values_packed, values_mid, values_land,
    fresh_rows, query_all, query_rows, fresh_all, result, rows_send, rows_land,
    slot_order, lengths, slot_of,
    scalar_sem, full_sem, fresh_sem, line_send, line_recv, chip_send, chip_recv,
    keys_send, keys_recv, mid_send, mid_recv, values_send, values_recv,
    small_send, small_recv, rows_send_sem, rows_recv_sem,
):
    s, h, b = lax.axis_index("section"), lax.axis_index("head"), lax.axis_index("batch")
    x, z = lax.div(s, 2), lax.div(h, 2)
    y_low = lax.rem(h, 2)
    y = lax.rem(s, 2) * 2 + y_low
    other = 1 - b
    sign = 1 - 2 * b
    mine = pl.ds(b * 16, 16)
    here = x * 4 + y
    here_mid = x * 4 + y_low * 2 + lax.div(y, 2)

    def remote(src, dst, send_sem, recv_sem, to):
        return pltpu.make_async_remote_copy(
            src_ref=src, dst_ref=dst, send_sem=send_sem, recv_sem=recv_sem,
            device_id=to, device_id_type=MESH,
        )

    def wait_for(ref, sem):
        pltpu.make_async_copy(ref, ref, sem).wait()

    def away(d, at, way):
        return lax.rem(at + way * d + 4, 4)

    def in_plane(at_x, at_y):
        return at_x * 2 + lax.div(at_y, 2), z * 2 + lax.rem(at_y, 2)

    def in_line(at_z):
        return at_z * 2 + y_low

    def owner_low(low):
        return lax.rem(y_low + low, 2)

    barrier = pltpu.get_barrier_semaphore()

    def greet(to):
        pl.semaphore_signal(barrier, inc=1, device_id=to, device_id_type=MESH)

    for dz in range(4):
        at_h = in_line(away(dz, z, 1))
        greet((s, at_h, other))
        if dz:
            greet((s, at_h, b))
    for low in (1, 0):
        for dx, dy in PLANE[low]:
            at_s, at_h = in_plane(away(dx, x, 1), away(dy, y, 1))
            greet((at_s, at_h, b))
            if low == 0:
                greet((at_s, at_h, other))

    scalars = [
        pltpu.make_async_copy(slot_order_hbm, slot_order, scalar_sem.at[0]),
        pltpu.make_async_copy(lengths_hbm, lengths, scalar_sem.at[1]),
    ]
    whole = [
        pltpu.make_async_copy(keys_flat.at[at], key_columns.at[:, pl.ds(at * HD, HD)], full_sem.at[0])
        for at in range(16)
    ]
    whole.append(pltpu.make_async_copy(values_flat, value_rows, full_sem.at[1]))
    fresh = [
        pltpu.make_async_copy(src, fresh_rows.at[n], fresh_sem.at[n])
        for n, src in enumerate((new_keys, new_values))
    ]
    for copy in scalars:
        copy.start()
    for low in (1, 0):
        pltpu.make_async_copy(
            values.at[:, :, owner_low(low), b], values_chip[low].at[mine], chip_recv.at[low]
        ).start()
    for low in (1, 0):
        pltpu.make_async_copy(
            keys.at[:, z, owner_low(low), b], keys_line[low].at[z, mine], line_recv.at[low]
        ).start()
    for copy in whole + fresh:
        copy.start()
    pl.semaphore_wait(barrier, 29)

    def swap(low):
        remote(
            values.at[:, :, owner_low(low), other], values_chip[low].at[mine],
            chip_send, chip_recv.at[low], (s, h, other),
        ).start()

    swap(1)

    def send_line(low, dz, to_b):
        to_z = away(dz, z, sign)
        remote(
            keys.at[:, to_z, owner_low(low), to_b], keys_line[low].at[z, mine],
            line_send, line_recv.at[low], (s, in_line(to_z), to_b),
        ).start()

    for low in (1, 0):
        for dz, to_b in ((1, b), (3, other), (2, b), (1, other), (3, b), (2, other), (0, other)):
            send_line(low, dz, to_b)

    head_rows = pl.ds(pl.multiple_of(h * GROUP * HD, GROUP * HD), GROUP * HD)
    head_cols = pl.ds(pl.multiple_of(h * HD, HD), HD)

    def small_pieces(to_s):
        return (
            (queries.at[:, to_s, :, head_rows], query_all.at[s]),
            (new_keys.at[:, to_s, :, head_cols], fresh_all.at[0, s]),
            (new_values.at[:, to_s, :, head_cols], fresh_all.at[1, s]),
        )

    def send_small(step, carry):
        to_s = lax.rem(s + step, 8)
        for n, (src, dst) in enumerate(small_pieces(to_s)):
            remote(src, dst, small_send.at[n], small_recv.at[n], (to_s, h, b)).start()
        return carry

    def pack_values(low):
        def step(at_s, carry):
            for k in range(4):
                values_packed[at_s * 2 + owner_low(low), :, k] = values_chip[low][slot_order[at_s * 4 + k]]
            return carry

        lax.fori_loop(0, 8, step, 0)

    def pack_keys(low):
        def step(at_s, carry):
            for k in range(4):
                slot = slot_order[at_s * 4 + k]
                for from_z in range(4):
                    keys_packed[at_s * 2 + owner_low(low), from_z, k] = keys_line[low][from_z, slot]
            return carry

        lax.fori_loop(0, 8, step, 0)

    def send_plane(packed, dx, dy, dst, send_sem, recv_sem):
        to_x, to_y = away(dx, x, sign), away(dy, y, sign)
        to_s, to_h = in_plane(to_x, to_y)
        remote(
            packed.at[to_x * 4 + to_y], dst, send_sem, recv_sem.at[group_of(dx, dy % 2)], (to_s, to_h, b)
        ).start()

    def take_values(low):
        wait_for(values_chip[low], chip_recv.at[low])
        if low == 1:
            swap(0)
        pack_values(low)

    def send_values(low):
        for dx, dy in PLANE[low]:
            send_plane(values_packed, dx, dy, values_mid.at[:, here_mid], mid_send, mid_recv)

    def forward_values(dx, low):
        group = group_of(dx, low)
        wait_for(values_mid.at[:, pl.ds(0, 2)], mid_recv.at[group])
        pair = pl.ds(away(dx, x, -sign) * 4 + owner_low(low) * 2, 2)
        for dz in (1, 3, 2):
            to_z = away(dz, z, sign)
            remote(
                values_mid.at[to_z, pair], values_land.at[z, pair],
                values_send, values_recv.at[group], (s, in_line(to_z), b),
            ).start()

    def turn_keys(low):
        wait_for(keys_line[low], line_recv.at[low])
        pack_keys(low)
        for dx, dy in PLANE[low]:
            send_plane(keys_packed, dx, dy, keys_land.at[here], keys_send, keys_recv)

    scalars[0].wait()
    scalars[1].wait()
    lax.fori_loop(1, 8, send_small, 0)
    for n, (src, dst) in enumerate(small_pieces(s)):
        pltpu.make_async_copy(src, dst, small_recv.at[n]).start()
    take_values(1)
    send_values(1)
    take_values(0)
    send_values(0)
    pltpu.make_async_copy(
        values_packed.at[here], values_mid.at[:, here_mid], mid_recv.at[group_of(0, 0)]
    ).start()

    for n, part in enumerate((query_all, fresh_all.at[0], fresh_all.at[1])):
        wait_for(part, small_recv.at[n])
    wait_for(key_columns, full_sem.at[0])
    wait_for(value_rows, full_sem.at[1])

    def spread_queries(at_s, carry):
        for t in range(2):
            rows = query_all[at_s, t].astype(F32)
            for g in range(GROUP):
                row = (g // 4) * 8 + t * 4 + g % 4
                for k in range(4):
                    query_rows[at_s * 4 + k, row : row + 1, :] = rows[k : k + 1, g * HD : g * HD + HD]
        return carry

    lax.fori_loop(0, 8, spread_queries, 0)

    def find_slot(at, carry):
        found = jnp.int32(0)
        for slot in range(32):
            found = jnp.where(slot_order[slot] == b * 16 + at, slot, found)
        slot_of[at] = found
        return carry

    lax.fori_loop(0, 16, find_slot, 0)

    lane = lax.broadcasted_iota(jnp.int32, (1, HD), 1)
    lane_prompt = lax.div(lane, 16)
    lane_later = lax.rem(lax.div(lane, 4), 2) == 1
    block_lane = lax.div(lax.broadcasted_iota(jnp.int32, (HD, HD), 1), 16)
    row4 = lax.broadcasted_iota(jnp.int32, (4, HD), 0)
    row512 = lax.broadcasted_iota(jnp.int32, (512, HD), 0)
    scale = HD ** -0.5

    def attend(first):
        slots = [slot_of[first + p] for p in range(8)]
        live = jnp.zeros((1, HD), jnp.int32)
        for p in range(8):
            live = jnp.where(lane_prompt == p, lengths[first + p + b * 16], live)

        def fresh_row(n, t, slot):
            rows = fresh_all[n, lax.div(slot, 4), t].astype(F32)
            return jnp.sum(jnp.where(row4 == lax.rem(slot, 4), rows, 0.0), axis=0, keepdims=True)

        questions = jnp.concatenate([query_rows[slot] for slot in slots], axis=0).T
        diagonal = jnp.concatenate(
            [jnp.where(block_lane == p, questions, 0.0) for p in range(8)], axis=0
        ).astype(BF16)
        fresh_keys = jnp.concatenate(
            [
                jnp.concatenate([fresh_row(0, 0, slot), fresh_row(0, 1, slot), jnp.zeros((14, HD), F32)], axis=0)
                for slot in slots
            ],
            axis=1,
        ).astype(BF16)
        scores = jnp.dot(
            key_columns[:, first * HD : (first + 8) * HD], diagonal, preferred_element_type=F32
        ) * scale
        fresh_scores = jnp.dot(fresh_keys, diagonal, preferred_element_type=F32) * scale
        kept = row512 < live
        scores = jnp.where(kept, scores, HIDDEN)
        n0 = fresh_scores[0:1]
        n1 = jnp.where(lane_later, fresh_scores[1:2], HIDDEN)
        peak = jnp.maximum(jnp.max(scores, axis=0, keepdims=True), jnp.maximum(n0, n1))
        mass = jnp.where(kept, jnp.exp(scores - peak), 0.0)
        m0 = jnp.exp(n0 - peak)
        m1 = jnp.where(lane_later, jnp.exp(n1 - peak), 0.0)
        total = jnp.sum(mass, axis=0, keepdims=True) + m0 + m1
        weights = mass.T.astype(BF16)
        m0, m1 = (m.astype(BF16).astype(F32) for m in (m0, m1))
        sides = jnp.concatenate([total, m0, m1, jnp.zeros((HD - 3, HD), F32)], axis=0).T
        for p, slot in enumerate(slots):
            cut = slice(p * 16, p * 16 + 16)
            weighted = jnp.dot(weights[cut], value_rows[first + p], preferred_element_type=F32)
            weighted += sides[cut, 1:2] * fresh_row(1, 0, slot)
            weighted += sides[cut, 2:3] * fresh_row(1, 1, slot)
            result[first + p] = weighted / sides[cut, 0:1]

    attend(0)
    attend(8)

    def hand_rows(at_s, carry):
        for pair in range(2):
            first, second = (
                result[jnp.clip(slot_order[at_s * 4 + pair * 2 + n] - b * 16, 0, 15)] for n in range(2)
            )
            for to_b in range(2):
                cut = slice(to_b * 8, to_b * 8 + 8)
                rows_send[at_s, to_b, pair] = jnp.concatenate((first[cut], second[cut]), axis=0).astype(BF16)
        return carry

    lax.fori_loop(0, 8, hand_rows, 0)

    def send_rows(to_s, to_b):
        remote(
            rows_send.at[to_s, to_b], rows_land.at[s, b], rows_send_sem, rows_recv_sem, (to_s, h, to_b)
        ).start()

    def send_rows_step(step, carry):
        to_s = lax.rem(s + step, 8)
        send_rows(to_s, b)
        send_rows(to_s, other)
        return carry

    lax.fori_loop(1, 8, send_rows_step, 0)
    send_rows(s, other)
    pltpu.make_async_copy(rows_send.at[s, b], rows_land.at[s, b], rows_recv_sem).start()
    owned = [slot_order[s * 4 + k] for k in range(4)]
    lives = [lengths[slot] for slot in owned]
    first_position = (h * 2 + b) * BLOCK
    position = first_position + lax.broadcasted_iota(jnp.int32, (BLOCK, HD), 0)
    for k in range(4):
        keep[k] = jnp.where(position < lives[k], 1.0, 0.0).astype(BF16)
    fresh[0].wait()
    fresh[1].wait()

    def place_fresh(layer, carry):
        wide = first_position + lax.broadcasted_iota(jnp.int32, (BLOCK, KVH * HD), 0)
        for n, out in enumerate((keys_fresh, values_cache)):
            new = [fresh_rows[n, t, layer].astype(F32) for t in range(2)]
            for k in range(4):
                rows = jnp.zeros((BLOCK, KVH * HD), F32)
                for t in range(2):
                    rows = jnp.where(wide == lives[k] + t, new[t][k : k + 1], rows)
                out[layer, k] = rows.astype(BF16)
        return carry

    lax.fori_loop(0, 8, place_fresh, 0)
    turn_keys(1)
    turn_keys(0)
    pltpu.make_async_copy(keys_packed.at[here], keys_land.at[here], keys_recv.at[group_of(0, 0)]).start()
    for low in (1, 0):
        for dx in (1, 3, 2, 0):
            forward_values(dx, low)

    def settle_values(src, from_x, low, from_z):
        def step(half, carry):
            from_low = owner_low(low)
            block = src.at[from_z, from_x * 4 + from_low * 2 + half]
            layer = from_x * 2 + half
            cut = pl.ds(pl.multiple_of((from_z * 2 + from_low) * HD, HD), HD)
            for k in range(4):
                values_cache[layer, k, :, cut] = jnp.where(keep[k] > 0, block[k], values_cache[layer, k, :, cut])
            return carry

        lax.fori_loop(0, 2, step, 0)

    owners = [lax.div(slot, 16) for slot in owned]

    def assemble(l, carry):
        picked = []
        for k in range(4):
            part = slice((k % 2) * 8, (k % 2) * 8 + 8)
            first, second = (rows_land[l, n, k // 2].astype(F32)[part] for n in range(2))
            picked.append(jnp.where(owners[k] == 0, first, second))
        for t in range(2):
            attention[t, l] = jnp.concatenate(
                [
                    jnp.concatenate([rows[t * 4 + g : t * 4 + g + 1] for rows in picked], axis=0)
                    for g in range(4)
                ],
                axis=1,
            ).astype(BF16)
        return carry

    for low in (1, 0):
        for dx in (1, 3, 2, 0):
            settle_values(values_mid, away(dx, x, -sign), low, z)
    wait_for(rows_land, rows_recv_sem)
    lax.fori_loop(0, 8, assemble, 0)
    for low in (1, 0):
        for dx in (1, 3, 2, 0):
            wait_for(values_land.at[pl.ds(0, 3), pl.ds(0, 2)], values_recv.at[group_of(dx, low)])
            for dz in (1, 3, 2):
                settle_values(values_land, away(dx, x, -sign), low, away(dz, z, -sign))
    for group in range(8):
        wait_for(keys_land.at[pl.ds(0, 2)], keys_recv.at[group])

    wait_for(value_rows.at[pl.ds(0, 8)], chip_send)
    wait_for(value_rows.at[pl.ds(0, 14)], line_send)
    for n, part in enumerate((query_all, fresh_all.at[0], fresh_all.at[1])):
        wait_for(part.at[pl.ds(0, 7)], small_send.at[n])
    wait_for(values_packed.at[pl.ds(0, 15)], mid_send)
    wait_for(keys_packed.at[pl.ds(0, 15)], keys_send)
    wait_for(values_land.at[pl.ds(0, 3)], values_send)
    wait_for(rows_send.at[pl.ds(0, 7)], rows_send_sem)
    wait_for(rows_send.at[0, 0], rows_send_sem)


def hand_out(
    attention, values, keys_land, keys_fresh, keep, attention_out, values_out, keys_out, keys, sem
):
    copies = [pltpu.make_async_copy(values.at[l], values_out.at[l], sem.at[l]) for l in range(8)]
    copies.append(pltpu.make_async_copy(attention, attention_out, sem.at[16]))
    for copy in copies:
        copy.start()
    kept = [keep[k] > 0 for k in range(4)]
    for l in range(8):
        for h in range(KVH):
            cut = slice(h * HD, h * HD + HD)
            for k in range(4):
                landed = keys_land[l // 2 * 4 + l % 2 * 2 + h % 2, h // 2, k]
                keys[l, k, :, cut] = jnp.where(kept[k], landed, keys_fresh[l, k, :, cut])
        copies.append(pltpu.make_async_copy(keys.at[l], keys_out.at[l], sem.at[8 + l]))
        copies[-1].start()
    for copy in copies:
        copy.wait()


def body(keys_prefill, values_prefill, lengths, slot_order, queries, new_keys, new_values):
    keys = keys_prefill.reshape(16, 4, 2, 2, BLOCK, HD)
    values = values_prefill.reshape(16, 4, 2, 2, BLOCK, HD)
    flat = (keys_prefill.reshape(16, 512, HD), values_prefill.reshape(16, 512, HD))
    any_spec = pl.BlockSpec(memory_space=pl.ANY)
    hbm_spec = pl.BlockSpec(memory_space=pltpu.HBM)
    vmem_spec = pl.BlockSpec(memory_space=pltpu.VMEM)
    dma, vmem = pltpu.SemaphoreType.DMA, pltpu.VMEM
    rows_shape, cache_shape = (2, 8, 4, 4 * HD), (8, 4, BLOCK, KVH * HD)
    plane_shape = (16, 4, 4, BLOCK, HD)
    plane, line = vmem(plane_shape, BF16), vmem((4, 16, 4, BLOCK, HD), BF16)

    def in_hbm(array):
        return pltpu.with_memory_space_constraint(array, pltpu.HBM)

    held = pl.pallas_call(
        relay,
        out_shape=tuple(
            vmem(shape, BF16) for shape in (rows_shape, cache_shape, plane_shape, cache_shape, (4, BLOCK, HD))
        ),
        in_specs=[hbm_spec] * 9,
        out_specs=(vmem_spec,) * 5,
        scratch_shapes=[
            vmem((512, 16 * HD), BF16), vmem((16, 512, HD), BF16),
            [vmem((4, 32, BLOCK, HD), BF16)] * 2, [vmem((32, 4, BLOCK, HD), BF16)] * 2,
            plane, plane, line, line,
            vmem((2, 2, 8, 4, KVH * HD), BF16), vmem((8, 2, 4, GROUP * HD), BF16), vmem((32, 16, HD), F32),
            vmem((2, 8, 2, 4, HD), BF16), vmem((16, 16, HD), F32),
            vmem((8, 2, 2, 16, HD), BF16), vmem((8, 2, 2, 16, HD), BF16),
            pltpu.SMEM((32,), jnp.int32), pltpu.SMEM((32,), jnp.int32), pltpu.SMEM((16,), jnp.int32),
            dma((2,)), dma((2,)), dma((2,)), dma, dma((2,)), dma, dma((2,)),
            dma, dma((8,)), dma, dma((8,)), dma, dma((8,)),
            dma((3,)), dma((3,)), dma, dma,
        ],
        compiler_params=pltpu.CompilerParams(
            collective_id=0, has_side_effects=True, vmem_limit_bytes=48 * 2**20
        ),
        name="relay",
    )(*(in_hbm(x) for x in (slot_order, lengths, keys, values, *flat, queries, new_keys, new_values)))
    attention, values_cache, keys_cache = pl.pallas_call(
        hand_out,
        out_shape=tuple(jax.ShapeDtypeStruct(shape, BF16) for shape in (rows_shape, cache_shape, cache_shape)),
        in_specs=[vmem_spec] * 5,
        out_specs=(any_spec,) * 3,
        scratch_shapes=[vmem(cache_shape, BF16), dma((17,))],
        compiler_params=pltpu.CompilerParams(vmem_limit_bytes=8 * 2**20),
        name="hand_out",
    )(*(pltpu.with_memory_space_constraint(x, pltpu.VMEM) for x in held))
    return attention, keys_cache, values_cache


def solution(mesh):
    in_specs = (
        P("section", "batch", None, "head"),
        P("section", "batch", None, "head"),
        P(),
        P(),
        P(None, None, "section", None),
        P(None, None, "section", None),
        P(None, None, "section", None),
    )
    out_specs = (
        P(None, None, "section", ("head", "batch")),
        P(None, "section", ("head", "batch"), None),
        P(None, "section", ("head", "batch"), None),
    )
    return jax.shard_map(body, mesh=mesh, in_specs=in_specs, out_specs=out_specs, check_vma=False)
```

profile of v0, /device:TPU:1, one launch (start us, length us, event | category | flops | bytes accessed | tf_op | source)
XLA Modules:
  0.0 62.7 jit_solution(18192151231408331402)
XLA Ops:
  0.6 59.9 %relay.1 = (bf16[2,8,4,512]{3,2,1,0:T(4,128)(2,1)S(1)}, bf16[8,4,32,1024]{3,2,1,0:T(8,128)(2,1)S(1)}, bf16[16,4,4,32,128]{4,3,2,1,0:T(8,128)(2,1)S(1)}, bf16[8,4...) custom-call(s32[32]{0:T(128)} %slot_order_hbm.1, s32[32]{0:T(128)} %lengths_hbm.1, ...), custom_call_target="tpu_custom_call" | custom-call | tf_op jit(solution)/shard_map/relay/pallas_call | solution.py:433
  60.6 2.2 %hand_out.1 = (bf16[2,8,4,512]{3,2,1,0:T(4,128)(2,1)}, bf16[8,4,32,1024]{3,2,1,0:T(8,128)(2,1)}, bf16[8,4,32,1024]{3,2,1,0:T(8,128)(2,1)}) custom-call(bf16[2,8,4,512]{3,2,1,0:T(4,128)(2,1)S(1)} %get-tuple-element.11.attention, bf16[8,4,32,1024]{3,2,1,0:T(8,128)(2,1)S(1)} %get-tuple-element.12.values, ...), custom_call_target="tpu_custom_call" | custom-call | tf_op jit(solution)/shard_map/hand_out/pallas_call | solution.py:457
where the time goes:
time: 62.8 us; the launch traced here: 62.7 us
  Pallas kernels  62.1 us (99%)
  between operations  0.64 us (1%)
    pallas_call x1, Pallas kernels, body(): pl.pallas_call(relay, out_shape=tuple((vmem(shape, BF16) for shape in (ro...  59.9 us
    pallas_call x1, Pallas kernels, body(): pl.pallas_call(hand_out, out_shape=tuple((jax.ShapeDtypeStruct(shape, BF1...  2.17 us

commit v1 on v0

--- a/solution.py
+++ b/solution.py
@@ -18,6 +18,9 @@
     1: ((1, 1), (3, 3), (1, 3), (3, 1), (2, 1), (0, 3), (2, 3), (0, 1)),
     0: ((1, 0), (0, 2), (3, 2), (1, 2), (3, 0), (2, 2), (2, 0)),
 }
+PIECES = ((1, 1), (1, 3), (1, 2), (0, 1), (0, 3), (0, 2), (1, 0), (0, 0))
+
+
 def group_of(dx, low):
     return low * 4 + dx
 
@@ -25,11 +28,11 @@
 def relay(
     slot_order_hbm, lengths_hbm, keys, values, keys_flat, values_flat, queries, new_keys, new_values,
     attention, values_cache, keys_land, keys_fresh, keep,
-    key_columns, value_rows, keys_line, values_chip, keys_packed, values_packed, values_mid, values_land,
+    key_columns, value_rows, keys_line, keys_near, values_chip, keys_packed, values_packed, values_mid, values_land,
     fresh_rows, query_all, query_rows, fresh_all, result, rows_send, rows_land,
     slot_order, lengths, slot_of,
-    scalar_sem, full_sem, fresh_sem, line_send, line_recv, chip_send, chip_recv,
-    keys_send, keys_recv, mid_send, mid_recv, values_send, values_recv,
+    scalar_sem, full_sem, fresh_sem, line_send, line_recv, near_recv, chip_send, chip_recv,
+    keys_send, keys_recv, mid_first, mid_send, mid_recv, mid_near, mid_near_recv, values_send, values_recv,
     small_send, small_recv, rows_send_sem, rows_recv_sem,
 ):
     s, h, b = lax.axis_index("section"), lax.axis_index("head"), lax.axis_index("batch")
@@ -95,36 +98,44 @@
     ]
     for copy in scalars:
         copy.start()
-    for low in (1, 0):
+    for piece, (low, dz) in enumerate(PIECES):
         pltpu.make_async_copy(
-            values.at[:, :, owner_low(low), b], values_chip[low].at[mine], chip_recv.at[low]
+            values.at[:, away(dz, z, sign), owner_low(low), b], values_chip[piece].at[mine], chip_recv.at[piece]
         ).start()
     for low in (1, 0):
         pltpu.make_async_copy(
-            keys.at[:, z, owner_low(low), b], keys_line[low].at[z, mine], line_recv.at[low]
+            keys.at[:, z, owner_low(low), b], keys_near[low].at[mine], near_recv.at[low]
         ).start()
     for copy in whole + fresh:
         copy.start()
     pl.semaphore_wait(barrier, 29)
 
-    def swap(low):
+    def swap(piece):
+        low, dz = PIECES[piece]
         remote(
-            values.at[:, :, owner_low(low), other], values_chip[low].at[mine],
-            chip_send, chip_recv.at[low], (s, h, other),
+            values.at[:, away(dz, z, -sign), owner_low(low), other], values_chip[piece].at[mine],
+            chip_send, chip_recv.at[piece], (s, h, other),
         ).start()
 
+    swap(0)
     swap(1)
 
     def send_line(low, dz, to_b):
         to_z = away(dz, z, sign)
+        d = away(dz, 0, sign)
         remote(
-            keys.at[:, to_z, owner_low(low), to_b], keys_line[low].at[z, mine],
+            keys.at[:, to_z, owner_low(low), to_b], keys_line[low].at[3 - d, mine],
             line_send, line_recv.at[low], (s, in_line(to_z), to_b),
         ).start()
 
     for low in (1, 0):
-        for dz, to_b in ((1, b), (3, other), (2, b), (1, other), (3, b), (2, other), (0, other)):
+        for dz, to_b in ((1, b), (3, other), (2, b), (1, other), (3, b), (2, other)):
             send_line(low, dz, to_b)
+    for low in (1, 0):
+        remote(
+            keys.at[:, z, owner_low(low), other], keys_near[low].at[mine],
+            line_send, near_recv.at[low], (s, h, other),
+        ).start()
 
     head_rows = pl.ds(pl.multiple_of(h * GROUP * HD, GROUP * HD), GROUP * HD)
     head_cols = pl.ds(pl.multiple_of(h * HD, HD), HD)
@@ -142,70 +153,86 @@
             remote(src, dst, small_send.at[n], small_recv.at[n], (to_s, h, b)).start()
         return carry
 
-    def pack_values(low):
+    def each_slot(do):
         def step(at_s, carry):
             for k in range(4):
-                values_packed[at_s * 2 + owner_low(low), :, k] = values_chip[low][slot_order[at_s * 4 + k]]
+                do(at_s, k, slot_order[at_s * 4 + k])
             return carry
 
         lax.fori_loop(0, 8, step, 0)
 
-    def pack_keys(low):
-        def step(at_s, carry):
-            for k in range(4):
-                slot = slot_order[at_s * 4 + k]
-                for from_z in range(4):
-                    keys_packed[at_s * 2 + owner_low(low), from_z, k] = keys_line[low][from_z, slot]
-            return carry
-
-        lax.fori_loop(0, 8, step, 0)
-
-    def send_plane(packed, dx, dy, dst, send_sem, recv_sem):
+    def send_plane(src, dx, dy, dst, send_sem, recv_sem):
         to_x, to_y = away(dx, x, sign), away(dy, y, sign)
         to_s, to_h = in_plane(to_x, to_y)
-        remote(
-            packed.at[to_x * 4 + to_y], dst, send_sem, recv_sem.at[group_of(dx, dy % 2)], (to_s, to_h, b)
-        ).start()
-
-    def take_values(low):
-        wait_for(values_chip[low], chip_recv.at[low])
-        if low == 1:
-            swap(0)
-        pack_values(low)
-
-    def send_values(low):
-        for dx, dy in PLANE[low]:
-            send_plane(values_packed, dx, dy, values_mid.at[:, here_mid], mid_send, mid_recv)
+        remote(src(to_x * 4 + to_y), dst, send_sem, recv_sem, (to_s, to_h, b)).start()
+
+    def take_values(piece):
+        low, dz = PIECES[piece]
+        at_z = away(dz, 0, sign)
+        wait_for(values_chip[piece], chip_recv.at[piece])
+        if piece + 2 < len(PIECES):
+            swap(piece + 2)
+
+        def pack(at_s, k, slot):
+            values_packed[at_s * 2 + owner_low(low), at_z, k] = values_chip[piece][slot]
+
+        each_slot(pack)
+        if dz:
+            for dx, dy in PLANE[low]:
+                send_plane(
+                    lambda to: values_packed.at[to, at_z], dx, dy, values_mid.at[at_z, here_mid],
+                    mid_first if low else mid_send, mid_recv.at[group_of(dx, low)],
+                )
+
+    far = pl.ds(1, 3)
 
     def forward_values(dx, low):
         group = group_of(dx, low)
-        wait_for(values_mid.at[:, pl.ds(0, 2)], mid_recv.at[group])
+        wait_for(values_mid.at[far, pl.ds(0, 2)], mid_recv.at[group])
         pair = pl.ds(away(dx, x, -sign) * 4 + owner_low(low) * 2, 2)
         for dz in (1, 3, 2):
-            to_z = away(dz, z, sign)
             remote(
-                values_mid.at[to_z, pair], values_land.at[z, pair],
-                values_send, values_recv.at[group], (s, in_line(to_z), b),
+                values_mid.at[dz, pair], values_land.at[dz - 1, pair],
+                values_send, values_recv.at[group], (s, in_line(away(dz, z, 1)), b),
             ).start()
+
+    def take_near_keys(low):
+        wait_for(keys_near[low], near_recv.at[low])
+
+        def pack(at_s, k, slot):
+            keys_packed[at_s * 2 + owner_low(low), 0, k] = keys_near[low][slot]
+
+        each_slot(pack)
+
+    def send_near(low):
+        for dx, dy in PLANE[low]:
+            send_plane(
+                lambda to: values_packed.at[to, 0], dx, dy, values_mid.at[0, here_mid], mid_near, mid_near_recv
+            )
+            send_plane(lambda to: keys_packed.at[to, 0], dx, dy, keys_land.at[here, 0], keys_send, keys_recv)
 
     def turn_keys(low):
         wait_for(keys_line[low], line_recv.at[low])
-        pack_keys(low)
+
+        def pack(at_s, k, slot):
+            for dz in range(1, 4):
+                keys_packed[at_s * 2 + owner_low(low), dz, k] = keys_line[low][dz - 1, slot]
+
+        each_slot(pack)
         for dx, dy in PLANE[low]:
-            send_plane(keys_packed, dx, dy, keys_land.at[here], keys_send, keys_recv)
+            send_plane(lambda to: keys_packed.at[to, far], dx, dy, keys_land.at[here, far], keys_send, keys_recv)
 
     scalars[0].wait()
     scalars[1].wait()
     lax.fori_loop(1, 8, send_small, 0)
     for n, (src, dst) in enumerate(small_pieces(s)):
         pltpu.make_async_copy(src, dst, small_recv.at[n]).start()
-    take_values(1)
-    send_values(1)
-    take_values(0)
-    send_values(0)
+    for piece in range(len(PIECES)):
+        take_values(piece)
     pltpu.make_async_copy(
-        values_packed.at[here], values_mid.at[:, here_mid], mid_recv.at[group_of(0, 0)]
+        values_packed.at[here, far], values_mid.at[far, here_mid], mid_recv.at[group_of(0, 0)]
     ).start()
+    pltpu.make_async_copy(values_packed.at[here, 0], values_mid.at[0, here_mid], mid_near_recv).start()
 
     for n, part in enumerate((query_all, fresh_all.at[0], fresh_all.at[1])):
         wait_for(part, small_recv.at[n])
@@ -334,17 +361,22 @@
         return carry
 
     lax.fori_loop(0, 8, place_fresh, 0)
+    take_near_keys(1)
+    take_near_keys(0)
+    wait_for(values_packed.at[pl.ds(0, 8), far], mid_first)
+    send_near(1)
+    send_near(0)
+    for low in (1, 0):
+        for dx in (1, 3, 2, 0):
+            forward_values(dx, low)
     turn_keys(1)
     turn_keys(0)
-    pltpu.make_async_copy(keys_packed.at[here], keys_land.at[here], keys_recv.at[group_of(0, 0)]).start()
-    for low in (1, 0):
-        for dx in (1, 3, 2, 0):
-            forward_values(dx, low)
-
-    def settle_values(src, from_x, low, from_z):
+    pltpu.make_async_copy(keys_packed.at[here], keys_land.at[here], keys_recv).start()
+
+    def settle_values(src, at, from_x, low, from_z):
         def step(half, carry):
             from_low = owner_low(low)
-            block = src.at[from_z, from_x * 4 + from_low * 2 + half]
+            block = src.at[at, from_x * 4 + from_low * 2 + half]
             layer = from_x * 2 + half
             cut = pl.ds(pl.multiple_of((from_z * 2 + from_low) * HD, HD), HD)
             for k in range(4):
@@ -371,26 +403,27 @@
             ).astype(BF16)
         return carry
 
-    for low in (1, 0):
-        for dx in (1, 3, 2, 0):
-            settle_values(values_mid, away(dx, x, -sign), low, z)
     wait_for(rows_land, rows_recv_sem)
     lax.fori_loop(0, 8, assemble, 0)
+    wait_for(values_mid.at[0], mid_near_recv)
     for low in (1, 0):
         for dx in (1, 3, 2, 0):
-            wait_for(values_land.at[pl.ds(0, 3), pl.ds(0, 2)], values_recv.at[group_of(dx, low)])
+            settle_values(values_mid, 0, away(dx, x, -sign), low, z)
+    for low in (1, 0):
+        for dx in (1, 3, 2, 0):
+            wait_for(values_land.at[:, pl.ds(0, 2)], values_recv.at[group_of(dx, low)])
             for dz in (1, 3, 2):
-                settle_values(values_land, away(dx, x, -sign), low, away(dz, z, -sign))
-    for group in range(8):
-        wait_for(keys_land.at[pl.ds(0, 2)], keys_recv.at[group])
+                settle_values(values_land, dz - 1, away(dx, x, -sign), low, away(dz, z, -1))
+    wait_for(keys_land, keys_recv)
 
     wait_for(value_rows.at[pl.ds(0, 8)], chip_send)
     wait_for(value_rows.at[pl.ds(0, 14)], line_send)
     for n, part in enumerate((query_all, fresh_all.at[0], fresh_all.at[1])):
         wait_for(part.at[pl.ds(0, 7)], small_send.at[n])
-    wait_for(values_packed.at[pl.ds(0, 15)], mid_send)
+    wait_for(values_packed.at[pl.ds(0, 7), far], mid_send)
+    wait_for(values_packed.at[pl.ds(0, 15), 0], mid_near)
     wait_for(keys_packed.at[pl.ds(0, 15)], keys_send)
-    wait_for(values_land.at[pl.ds(0, 3)], values_send)
+    wait_for(values_land, values_send)
     wait_for(rows_send.at[pl.ds(0, 7)], rows_send_sem)
     wait_for(rows_send.at[0, 0], rows_send_sem)
 
@@ -403,11 +436,12 @@
     for copy in copies:
         copy.start()
     kept = [keep[k] > 0 for k in range(4)]
+    z = lax.div(lax.axis_index("head"), 2)
     for l in range(8):
         for h in range(KVH):
             cut = slice(h * HD, h * HD + HD)
             for k in range(4):
-                landed = keys_land[l // 2 * 4 + l % 2 * 2 + h % 2, h // 2, k]
+                landed = keys_land[l // 2 * 4 + l % 2 * 2 + h % 2, lax.rem(h // 2 - z + 4, 4), k]
                 keys[l, k, :, cut] = jnp.where(kept[k], landed, keys_fresh[l, k, :, cut])
         copies.append(pltpu.make_async_copy(keys.at[l], keys_out.at[l], sem.at[8 + l]))
         copies[-1].start()
@@ -425,7 +459,6 @@
     dma, vmem = pltpu.SemaphoreType.DMA, pltpu.VMEM
     rows_shape, cache_shape = (2, 8, 4, 4 * HD), (8, 4, BLOCK, KVH * HD)
     plane_shape = (16, 4, 4, BLOCK, HD)
-    plane, line = vmem(plane_shape, BF16), vmem((4, 16, 4, BLOCK, HD), BF16)
 
     def in_hbm(array):
         return pltpu.with_memory_space_constraint(array, pltpu.HBM)
@@ -439,14 +472,16 @@
         out_specs=(vmem_spec,) * 5,
         scratch_shapes=[
             vmem((512, 16 * HD), BF16), vmem((16, 512, HD), BF16),
-            [vmem((4, 32, BLOCK, HD), BF16)] * 2, [vmem((32, 4, BLOCK, HD), BF16)] * 2,
-            plane, plane, line, line,
+            [vmem((3, 32, BLOCK, HD), BF16)] * 2, [vmem((32, BLOCK, HD), BF16)] * 2,
+            [vmem((32, BLOCK, HD), BF16)] * len(PIECES),
+            vmem(plane_shape, BF16), vmem(plane_shape, BF16),
+            vmem((4, 16, 4, BLOCK, HD), BF16), vmem((3, 16, 4, BLOCK, HD), BF16),
             vmem((2, 2, 8, 4, KVH * HD), BF16), vmem((8, 2, 4, GROUP * HD), BF16), vmem((32, 16, HD), F32),
             vmem((2, 8, 2, 4, HD), BF16), vmem((16, 16, HD), F32),
             vmem((8, 2, 2, 16, HD), BF16), vmem((8, 2, 2, 16, HD), BF16),
             pltpu.SMEM((32,), jnp.int32), pltpu.SMEM((32,), jnp.int32), pltpu.SMEM((16,), jnp.int32),
-            dma((2,)), dma((2,)), dma((2,)), dma, dma((2,)), dma, dma((2,)),
-            dma, dma((8,)), dma, dma((8,)), dma, dma((8,)),
+            dma((2,)), dma((2,)), dma((2,)), dma, dma((2,)), dma((2,)), dma, dma((len(PIECES),)),
+            dma, dma, dma, dma, dma((8,)), dma, dma, dma, dma((8,)),
             dma((3,)), dma((3,)), dma, dma,
         ],
         compiler_params=pltpu.CompilerParams(

time: 62.8 us -> 61.6 us (0.981)
  Pallas kernels: 62.1 us -> 60.8 us
    pallas_call x1, Pallas kernels: 59.9 us -> 58.7 us  [body(): pl.pallas_call(relay, out_shape=tuple((vmem(shape, BF16) for shape in (ro...]
where the time goes in v1:
time: 61.6 us; the launch traced here: 61.5 us
  Pallas kernels  60.8 us (99%)
  between operations  0.64 us (1%)
    pallas_call x1, Pallas kernels, body(): pl.pallas_call(relay, out_shape=tuple((vmem(shape, BF16) for shape in (ro...  58.7 us
    pallas_call x1, Pallas kernels, body(): pl.pallas_call(hand_out, out_shape=tuple((jax.ShapeDtypeStruct(shape, BF1...  2.17 us

profile of v1, /device:TPU:1, one launch (start us, length us, event | category | flops | bytes accessed | tf_op | source)
XLA Modules:
  0.0 61.5 jit_solution(15580540304916130647)
XLA Ops:
  0.6 58.7 %relay.1 = (bf16[2,8,4,512]{3,2,1,0:T(4,128)(2,1)S(1)}, bf16[8,4,32,1024]{3,2,1,0:T(8,128)(2,1)S(1)}, bf16[16,4,4,32,128]{4,3,2,1,0:T(8,128)(2,1)S(1)}, bf16[8,4...) custom-call(s32[32]{0:T(128)} %slot_order_hbm.1, s32[32]{0:T(128)} %lengths_hbm.1, ...), custom_call_target="tpu_custom_call" | custom-call | tf_op jit(solution)/shard_map/relay/pallas_call | solution.py:466
  59.3 2.2 %hand_out.1 = (bf16[2,8,4,512]{3,2,1,0:T(4,128)(2,1)}, bf16[8,4,32,1024]{3,2,1,0:T(8,128)(2,1)}, bf16[8,4,32,1024]{3,2,1,0:T(8,128)(2,1)}) custom-call(bf16[2,8,4,512]{3,2,1,0:T(4,128)(2,1)S(1)} %get-tuple-element.11.attention, bf16[8,4,32,1024]{3,2,1,0:T(8,128)(2,1)S(1)} %get-tuple-element.12.values, ...), custom_call_target="tpu_custom_call" | custom-call | tf_op jit(solution)/shard_map/hand_out/pallas_call | solution.py:492

commit v2 on v1

--- a/solution.py
+++ b/solution.py
@@ -32,7 +32,7 @@
     fresh_rows, query_all, query_rows, fresh_all, result, rows_send, rows_land,
     slot_order, lengths, slot_of,
     scalar_sem, full_sem, fresh_sem, line_send, line_recv, near_recv, chip_send, chip_recv,
-    keys_send, keys_recv, mid_first, mid_send, mid_recv, mid_near, mid_near_recv, values_send, values_recv,
+    keys_send, keys_recv, mid_send, mid_recv, mid_near, mid_near_recv, values_send, values_recv,
     small_send, small_recv, rows_send_sem, rows_recv_sem,
 ):
     s, h, b = lax.axis_index("section"), lax.axis_index("head"), lax.axis_index("batch")
@@ -181,7 +181,7 @@
             for dx, dy in PLANE[low]:
                 send_plane(
                     lambda to: values_packed.at[to, at_z], dx, dy, values_mid.at[at_z, here_mid],
-                    mid_first if low else mid_send, mid_recv.at[group_of(dx, low)],
+                    mid_send, mid_recv.at[group_of(dx, low)],
                 )
 
     far = pl.ds(1, 3)
@@ -204,11 +204,14 @@
 
         each_slot(pack)
 
-    def send_near(low):
-        for dx, dy in PLANE[low]:
+    def send_near_values():
+        for dx, dy in PLANE[1] + PLANE[0]:
             send_plane(
                 lambda to: values_packed.at[to, 0], dx, dy, values_mid.at[0, here_mid], mid_near, mid_near_recv
             )
+
+    def send_near_keys():
+        for dx, dy in PLANE[1] + PLANE[0]:
             send_plane(lambda to: keys_packed.at[to, 0], dx, dy, keys_land.at[here, 0], keys_send, keys_recv)
 
     def turn_keys(low):
@@ -363,12 +366,12 @@
     lax.fori_loop(0, 8, place_fresh, 0)
     take_near_keys(1)
     take_near_keys(0)
-    wait_for(values_packed.at[pl.ds(0, 8), far], mid_first)
-    send_near(1)
-    send_near(0)
-    for low in (1, 0):
-        for dx in (1, 3, 2, 0):
-            forward_values(dx, low)
+    for dx in (1, 3, 2, 0):
+        forward_values(dx, 1)
+    send_near_values()
+    for dx in (1, 3, 2, 0):
+        forward_values(dx, 0)
+    send_near_keys()
     turn_keys(1)
     turn_keys(0)
     pltpu.make_async_copy(keys_packed.at[here], keys_land.at[here], keys_recv).start()
@@ -420,7 +423,7 @@
     wait_for(value_rows.at[pl.ds(0, 14)], line_send)
     for n, part in enumerate((query_all, fresh_all.at[0], fresh_all.at[1])):
         wait_for(part.at[pl.ds(0, 7)], small_send.at[n])
-    wait_for(values_packed.at[pl.ds(0, 7), far], mid_send)
+    wait_for(values_packed.at[pl.ds(0, 15), far], mid_send)
     wait_for(values_packed.at[pl.ds(0, 15), 0], mid_near)
     wait_for(keys_packed.at[pl.ds(0, 15)], keys_send)
     wait_for(values_land, values_send)
@@ -481,7 +484,7 @@
             vmem((8, 2, 2, 16, HD), BF16), vmem((8, 2, 2, 16, HD), BF16),
             pltpu.SMEM((32,), jnp.int32), pltpu.SMEM((32,), jnp.int32), pltpu.SMEM((16,), jnp.int32),
             dma((2,)), dma((2,)), dma((2,)), dma, dma((2,)), dma((2,)), dma, dma((len(PIECES),)),
-            dma, dma, dma, dma, dma((8,)), dma, dma, dma, dma((8,)),
+            dma, dma, dma, dma((8,)), dma, dma, dma, dma((8,)),
             dma((3,)), dma((3,)), dma, dma,
         ],
         compiler_params=pltpu.CompilerParams(

time: 61.6 us -> 61.5 us (level)
  no operation moved by 1% of the time
where the time goes in v2:
time: 61.5 us; the launch traced here: 61.4 us
  Pallas kernels  60.7 us (99%)
  between operations  0.64 us (1%)
    pallas_call x1, Pallas kernels, body(): pl.pallas_call(relay, out_shape=tuple((vmem(shape, BF16) for shape in (ro...  58.5 us
    pallas_call x1, Pallas kernels, body(): pl.pallas_call(hand_out, out_shape=tuple((jax.ShapeDtypeStruct(shape, BF1...  2.17 us

profile of v2, /device:TPU:1, one launch (start us, length us, event | category | flops | bytes accessed | tf_op | source)
XLA Modules:
  0.0 61.4 jit_solution(1231151796221181848)
XLA Ops:
  0.6 58.5 %relay.1 = (bf16[2,8,4,512]{3,2,1,0:T(4,128)(2,1)S(1)}, bf16[8,4,32,1024]{3,2,1,0:T(8,128)(2,1)S(1)}, bf16[16,4,4,32,128]{4,3,2,1,0:T(8,128)(2,1)S(1)}, bf16[8,4...) custom-call(s32[32]{0:T(128)} %slot_order_hbm.1, s32[32]{0:T(128)} %lengths_hbm.1, ...), custom_call_target="tpu_custom_call" | custom-call | tf_op jit(solution)/shard_map/relay/pallas_call | solution.py:469
  59.2 2.2 %hand_out.1 = (bf16[2,8,4,512]{3,2,1,0:T(4,128)(2,1)}, bf16[8,4,32,1024]{3,2,1,0:T(8,128)(2,1)}, bf16[8,4,32,1024]{3,2,1,0:T(8,128)(2,1)}) custom-call(bf16[2,8,4,512]{3,2,1,0:T(4,128)(2,1)S(1)} %get-tuple-element.11.attention, bf16[8,4,32,1024]{3,2,1,0:T(8,128)(2,1)S(1)} %get-tuple-element.12.values, ...), custom_call_target="tpu_custom_call" | custom-call | tf_op jit(solution)/shard_map/hand_out/pallas_call | solution.py:495

commit v3 on v2

--- a/solution.py
+++ b/solution.py
@@ -123,10 +123,12 @@
     def send_line(low, dz, to_b):
         to_z = away(dz, z, sign)
         d = away(dz, 0, sign)
-        remote(
-            keys.at[:, to_z, owner_low(low), to_b], keys_line[low].at[3 - d, mine],
-            line_send, line_recv.at[low], (s, in_line(to_z), to_b),
-        ).start()
+        for half in range(2):
+            remote(
+                keys.at[pl.ds(half * 8, 8), to_z, owner_low(low), to_b],
+                keys_line[low].at[3 - d, pl.ds(b * 16 + half * 8, 8)],
+                line_send, line_recv.at[low], (s, in_line(to_z), to_b),
+            ).start()
 
     for low in (1, 0):
         for dz, to_b in ((1, b), (3, other), (2, b), (1, other), (3, b), (2, other)):
@@ -189,12 +191,13 @@
     def forward_values(dx, low):
         group = group_of(dx, low)
         wait_for(values_mid.at[far, pl.ds(0, 2)], mid_recv.at[group])
-        pair = pl.ds(away(dx, x, -sign) * 4 + owner_low(low) * 2, 2)
-        for dz in (1, 3, 2):
-            remote(
-                values_mid.at[dz, pair], values_land.at[dz - 1, pair],
-                values_send, values_recv.at[group], (s, in_line(away(dz, z, 1)), b),
-            ).start()
+        first = away(dx, x, -sign) * 4 + owner_low(low) * 2
+        for at in range(2):
+            for dz in (1, 3, 2):
+                remote(
+                    values_mid.at[dz, first + at], values_land.at[dz - 1, first + at],
+                    values_send, values_recv.at[group], (s, in_line(away(dz, z, 1)), b),
+                ).start()
 
     def take_near_keys(low):
         wait_for(keys_near[low], near_recv.at[low])
@@ -223,7 +226,8 @@
 
         each_slot(pack)
         for dx, dy in PLANE[low]:
-            send_plane(lambda to: keys_packed.at[to, far], dx, dy, keys_land.at[here, far], keys_send, keys_recv)
+            for dz in range(1, 4):
+                send_plane(lambda to: keys_packed.at[to, dz], dx, dy, keys_land.at[here, dz], keys_send, keys_recv)
 
     scalars[0].wait()
     scalars[1].wait()

time: 61.5 us -> 61.4 us (level)
  no operation moved by 1% of the time
where the time goes in v3:
time: 61.4 us; the launch traced here: 61.3 us
  Pallas kernels  60.7 us (99%)
  between operations  0.64 us (1%)
    pallas_call x1, Pallas kernels, body(): pl.pallas_call(relay, out_shape=tuple((vmem(shape, BF16) for shape in (ro...  58.5 us
    pallas_call x1, Pallas kernels, body(): pl.pallas_call(hand_out, out_shape=tuple((jax.ShapeDtypeStruct(shape, BF1...  2.17 us

profile of v3, /device:TPU:1, one launch (start us, length us, event | category | flops | bytes accessed | tf_op | source)
XLA Modules:
  0.0 61.3 jit_solution(11297055126879460869)
XLA Ops:
  0.6 58.5 %relay.1 = (bf16[2,8,4,512]{3,2,1,0:T(4,128)(2,1)S(1)}, bf16[8,4,32,1024]{3,2,1,0:T(8,128)(2,1)S(1)}, bf16[16,4,4,32,128]{4,3,2,1,0:T(8,128)(2,1)S(1)}, bf16[8,4...) custom-call(s32[32]{0:T(128)} %slot_order_hbm.1, s32[32]{0:T(128)} %lengths_hbm.1, ...), custom_call_target="tpu_custom_call" | custom-call | tf_op jit(solution)/shard_map/relay/pallas_call | solution.py:473
  59.1 2.2 %hand_out.1 = (bf16[2,8,4,512]{3,2,1,0:T(4,128)(2,1)}, bf16[8,4,32,1024]{3,2,1,0:T(8,128)(2,1)}, bf16[8,4,32,1024]{3,2,1,0:T(8,128)(2,1)}) custom-call(bf16[2,8,4,512]{3,2,1,0:T(4,128)(2,1)S(1)} %get-tuple-element.11.attention, bf16[8,4,32,1024]{3,2,1,0:T(8,128)(2,1)S(1)} %get-tuple-element.12.values, ...), custom_call_target="tpu_custom_call" | custom-call | tf_op jit(solution)/shard_map/hand_out/pallas_call | solution.py:499

commit v4 on v2

--- a/solution.py
+++ b/solution.py
@@ -27,8 +27,8 @@
 
 def relay(
     slot_order_hbm, lengths_hbm, keys, values, keys_flat, values_flat, queries, new_keys, new_values,
-    attention, values_cache, keys_land, keys_fresh, keep,
-    key_columns, value_rows, keys_line, keys_near, values_chip, keys_packed, values_packed, values_mid, values_land,
+    attention, keys_land, values_land, keys_fresh, values_fresh, keep,
+    key_columns, value_rows, keys_line, keys_near, values_chip, keys_packed, values_packed, values_mid,
     fresh_rows, query_all, query_rows, fresh_all, result, rows_send, rows_land,
     slot_order, lengths, slot_of,
     scalar_sem, full_sem, fresh_sem, line_send, line_recv, near_recv, chip_send, chip_recv,
@@ -180,7 +180,7 @@
         if dz:
             for dx, dy in PLANE[low]:
                 send_plane(
-                    lambda to: values_packed.at[to, at_z], dx, dy, values_mid.at[at_z, here_mid],
+                    lambda to: values_packed.at[to, at_z], dx, dy, values_mid.at[at_z - 1, here_mid],
                     mid_send, mid_recv.at[group_of(dx, low)],
                 )
 
@@ -188,12 +188,12 @@
 
     def forward_values(dx, low):
         group = group_of(dx, low)
-        wait_for(values_mid.at[far, pl.ds(0, 2)], mid_recv.at[group])
+        wait_for(values_mid.at[:, pl.ds(0, 2)], mid_recv.at[group])
         pair = pl.ds(away(dx, x, -sign) * 4 + owner_low(low) * 2, 2)
         for dz in (1, 3, 2):
             remote(
-                values_mid.at[dz, pair], values_land.at[dz - 1, pair],
-                values_send, values_recv.at[group], (s, in_line(away(dz, z, 1)), b),
+                values_mid.at[dz - 1, pair], values_land.at[dz, pair],
+                values_send, values_recv, (s, in_line(away(dz, z, 1)), b),
             ).start()
 
     def take_near_keys(low):
@@ -207,7 +207,7 @@
     def send_near_values():
         for dx, dy in PLANE[1] + PLANE[0]:
             send_plane(
-                lambda to: values_packed.at[to, 0], dx, dy, values_mid.at[0, here_mid], mid_near, mid_near_recv
+                lambda to: values_packed.at[to, 0], dx, dy, values_land.at[0, here_mid], mid_near, mid_near_recv
             )
 
     def send_near_keys():
@@ -233,9 +233,9 @@
     for piece in range(len(PIECES)):
         take_values(piece)
     pltpu.make_async_copy(
-        values_packed.at[here, far], values_mid.at[far, here_mid], mid_recv.at[group_of(0, 0)]
+        values_packed.at[here, far], values_mid.at[:, here_mid], mid_recv.at[group_of(0, 0)]
     ).start()
-    pltpu.make_async_copy(values_packed.at[here, 0], values_mid.at[0, here_mid], mid_near_recv).start()
+    pltpu.make_async_copy(values_packed.at[here, 0], values_land.at[0, here_mid], mid_near_recv).start()
 
     for n, part in enumerate((query_all, fresh_all.at[0], fresh_all.at[1])):
         wait_for(part, small_recv.at[n])
@@ -354,7 +354,7 @@
 
     def place_fresh(layer, carry):
         wide = first_position + lax.broadcasted_iota(jnp.int32, (BLOCK, KVH * HD), 0)
-        for n, out in enumerate((keys_fresh, values_cache)):
+        for n, out in enumerate((keys_fresh, values_fresh)):
             new = [fresh_rows[n, t, layer].astype(F32) for t in range(2)]
             for k in range(4):
                 rows = jnp.zeros((BLOCK, KVH * HD), F32)
@@ -375,18 +375,6 @@
     turn_keys(1)
     turn_keys(0)
     pltpu.make_async_copy(keys_packed.at[here], keys_land.at[here], keys_recv).start()
-
-    def settle_values(src, at, from_x, low, from_z):
-        def step(half, carry):
-            from_low = owner_low(low)
-            block = src.at[at, from_x * 4 + from_low * 2 + half]
-            layer = from_x * 2 + half
-            cut = pl.ds(pl.multiple_of((from_z * 2 + from_low) * HD, HD), HD)
-            for k in range(4):
-                values_cache[layer, k, :, cut] = jnp.where(keep[k] > 0, block[k], values_cache[layer, k, :, cut])
-            return carry
-
-        lax.fori_loop(0, 2, step, 0)
 
     owners = [lax.div(slot, 16) for slot in owned]
 
@@ -408,15 +396,8 @@
 
     wait_for(rows_land, rows_recv_sem)
     lax.fori_loop(0, 8, assemble, 0)
-    wait_for(values_mid.at[0], mid_near_recv)
-    for low in (1, 0):
-        for dx in (1, 3, 2, 0):
-            settle_values(values_mid, 0, away(dx, x, -sign), low, z)
-    for low in (1, 0):
-        for dx in (1, 3, 2, 0):
-            wait_for(values_land.at[:, pl.ds(0, 2)], values_recv.at[group_of(dx, low)])
-            for dz in (1, 3, 2):
-                settle_values(values_land, dz - 1, away(dx, x, -sign), low, away(dz, z, -1))
+    wait_for(values_land.at[0], mid_near_recv)
+    wait_for(values_land.at[far], values_recv)
     wait_for(keys_land, keys_recv)
 
     wait_for(value_rows.at[pl.ds(0, 8)], chip_send)
@@ -426,28 +407,32 @@
     wait_for(values_packed.at[pl.ds(0, 15), far], mid_send)
     wait_for(values_packed.at[pl.ds(0, 15), 0], mid_near)
     wait_for(keys_packed.at[pl.ds(0, 15)], keys_send)
-    wait_for(values_land, values_send)
+    wait_for(values_mid, values_send)
     wait_for(rows_send.at[pl.ds(0, 7)], rows_send_sem)
     wait_for(rows_send.at[0, 0], rows_send_sem)
 
 
 def hand_out(
-    attention, values, keys_land, keys_fresh, keep, attention_out, values_out, keys_out, keys, sem
+    attention, keys_land, values_land, keys_fresh, values_fresh, keep,
+    attention_out, keys_out, values_out, keys, values, sem,
 ):
-    copies = [pltpu.make_async_copy(values.at[l], values_out.at[l], sem.at[l]) for l in range(8)]
-    copies.append(pltpu.make_async_copy(attention, attention_out, sem.at[16]))
-    for copy in copies:
-        copy.start()
+    copies = [pltpu.make_async_copy(attention, attention_out, sem.at[16])]
+    copies[0].start()
     kept = [keep[k] > 0 for k in range(4)]
     z = lax.div(lax.axis_index("head"), 2)
     for l in range(8):
+        x, y_high = l // 2, l % 2
         for h in range(KVH):
             cut = slice(h * HD, h * HD + HD)
+            from_z, y_low = h // 2, h % 2
             for k in range(4):
-                landed = keys_land[l // 2 * 4 + l % 2 * 2 + h % 2, lax.rem(h // 2 - z + 4, 4), k]
+                landed = keys_land[x * 4 + y_high * 2 + y_low, lax.rem(from_z - z + 4, 4), k]
                 keys[l, k, :, cut] = jnp.where(kept[k], landed, keys_fresh[l, k, :, cut])
-        copies.append(pltpu.make_async_copy(keys.at[l], keys_out.at[l], sem.at[8 + l]))
-        copies[-1].start()
+                landed = values_land[lax.rem(z - from_z + 4, 4), x * 4 + y_low * 2 + y_high, k]
+                values[l, k, :, cut] = jnp.where(kept[k], landed, values_fresh[l, k, :, cut])
+        for n, (src, dst) in enumerate(((keys, keys_out), (values, values_out))):
+            copies.append(pltpu.make_async_copy(src.at[l], dst.at[l], sem.at[n * 8 + l]))
+            copies[-1].start()
     for copy in copies:
         copy.wait()
 
@@ -461,7 +446,7 @@
     vmem_spec = pl.BlockSpec(memory_space=pltpu.VMEM)
     dma, vmem = pltpu.SemaphoreType.DMA, pltpu.VMEM
     rows_shape, cache_shape = (2, 8, 4, 4 * HD), (8, 4, BLOCK, KVH * HD)
-    plane_shape = (16, 4, 4, BLOCK, HD)
+    plane_shape, line_shape = (16, 4, 4, BLOCK, HD), (4, 16, 4, BLOCK, HD)
 
     def in_hbm(array):
         return pltpu.with_memory_space_constraint(array, pltpu.HBM)
@@ -469,22 +454,22 @@
     held = pl.pallas_call(
         relay,
         out_shape=tuple(
-            vmem(shape, BF16) for shape in (rows_shape, cache_shape, plane_shape, cache_shape, (4, BLOCK, HD))
+            vmem(shape, BF16) for shape in (rows_shape, plane_shape, line_shape, cache_shape, cache_shape, (4, BLOCK, HD))
         ),
         in_specs=[hbm_spec] * 9,
-        out_specs=(vmem_spec,) * 5,
+        out_specs=(vmem_spec,) * 6,
         scratch_shapes=[
             vmem((512, 16 * HD), BF16), vmem((16, 512, HD), BF16),
             [vmem((3, 32, BLOCK, HD), BF16)] * 2, [vmem((32, BLOCK, HD), BF16)] * 2,
             [vmem((32, BLOCK, HD), BF16)] * len(PIECES),
             vmem(plane_shape, BF16), vmem(plane_shape, BF16),
-            vmem((4, 16, 4, BLOCK, HD), BF16), vmem((3, 16, 4, BLOCK, HD), BF16),
+            vmem((3, 16, 4, BLOCK, HD), BF16),
             vmem((2, 2, 8, 4, KVH * HD), BF16), vmem((8, 2, 4, GROUP * HD), BF16), vmem((32, 16, HD), F32),
             vmem((2, 8, 2, 4, HD), BF16), vmem((16, 16, HD), F32),
             vmem((8, 2, 2, 16, HD), BF16), vmem((8, 2, 2, 16, HD), BF16),
             pltpu.SMEM((32,), jnp.int32), pltpu.SMEM((32,), jnp.int32), pltpu.SMEM((16,), jnp.int32),
             dma((2,)), dma((2,)), dma((2,)), dma, dma((2,)), dma((2,)), dma, dma((len(PIECES),)),
-            dma, dma, dma, dma((8,)), dma, dma, dma, dma((8,)),
+            dma, dma, dma, dma((8,)), dma, dma, dma, dma,
             dma((3,)), dma((3,)), dma, dma,
         ],
         compiler_params=pltpu.CompilerParams(
@@ -492,16 +477,15 @@
         ),
         name="relay",
     )(*(in_hbm(x) for x in (slot_order, lengths, keys, values, *flat, queries, new_keys, new_values)))
-    attention, values_cache, keys_cache = pl.pallas_call(
+    return pl.pallas_call(
         hand_out,
         out_shape=tuple(jax.ShapeDtypeStruct(shape, BF16) for shape in (rows_shape, cache_shape, cache_shape)),
-        in_specs=[vmem_spec] * 5,
+        in_specs=[vmem_spec] * 6,
         out_specs=(any_spec,) * 3,
-        scratch_shapes=[vmem(cache_shape, BF16), dma((17,))],
+        scratch_shapes=[vmem(cache_shape, BF16), vmem(cache_shape, BF16), dma((17,))],
         compiler_params=pltpu.CompilerParams(vmem_limit_bytes=8 * 2**20),
         name="hand_out",
     )(*(pltpu.with_memory_space_constraint(x, pltpu.VMEM) for x in held))
-    return attention, keys_cache, values_cache
 
 
 def solution(mesh):

time: 61.5 us -> 61.5 us (level)
  no operation moved by 1% of the time
where the time goes in v4:
time: 61.5 us; the launch traced here: 61.4 us
  Pallas kernels  60.8 us (99%)
  between operations  0.64 us (1%)
    pallas_call x1, Pallas kernels, body(): pl.pallas_call(relay, out_shape=tuple((vmem(shape, BF16) for shape in (ro...  58.5 us
    pallas_call x1, Pallas kernels, body(): pl.pallas_call(hand_out, out_shape=tuple((jax.ShapeDtypeStruct(shape, BF1...  2.31 us

profile of v4, /device:TPU:1, one launch (start us, length us, event | category | flops | bytes accessed | tf_op | source)
XLA Modules:
  0.0 61.4 jit_solution(17640977475044857509)
XLA Ops:
  0.6 58.5 %relay.1 = (bf16[2,8,4,512]{3,2,1,0:T(4,128)(2,1)S(1)}, bf16[16,4,4,32,128]{4,3,2,1,0:T(8,128)(2,1)S(1)}, bf16[4,16,4,32,128]{4,3,2,1,0:T(8,128)(2,1)S(1)}, bf16...) custom-call(s32[32]{0:T(128)} %slot_order_hbm.1, ...), custom_call_target="tpu_custom_call" | custom-call | tf_op jit(solution)/shard_map/relay/pallas_call | solution.py:454
  59.1 2.3 %hand_out.1 = (bf16[2,8,4,512]{3,2,1,0:T(4,128)(2,1)}, bf16[8,4,32,1024]{3,2,1,0:T(8,128)(2,1)}, bf16[8,4,32,1024]{3,2,1,0:T(8,128)(2,1)}) custom-call(bf16[2,8,4,512]{3,2,1,0:T(4,128)(2,1)S(1)} %get-tuple-element.9.attention, bf16[16,4,4,32,128]{4,3,2,1,0:T(8,128)(2,1)S(1)} %get-tuple-element.10.keys_land, ...), custom_call_target="tpu_custom_call" | custom-call | tf_op jit(solution)/shard_map/hand_out/pallas_call | solution.py:480

commit v5 on v4

--- a/solution.py
+++ b/solution.py
@@ -29,11 +29,11 @@
     slot_order_hbm, lengths_hbm, keys, values, keys_flat, values_flat, queries, new_keys, new_values,
     attention, keys_land, values_land, keys_fresh, values_fresh, keep,
     key_columns, value_rows, keys_line, keys_near, values_chip, keys_packed, values_packed, values_mid,
-    fresh_rows, query_all, query_rows, fresh_all, result, rows_send, rows_land,
+    fresh_rows, query_all, query_rows, fresh_all, result, rows_mine, rows_swap, rows_send, rows_land,
     slot_order, lengths, slot_of,
     scalar_sem, full_sem, fresh_sem, line_send, line_recv, near_recv, chip_send, chip_recv,
     keys_send, keys_recv, mid_send, mid_recv, mid_near, mid_near_recv, values_send, values_recv,
-    small_send, small_recv, rows_send_sem, rows_recv_sem,
+    small_send, small_recv, share_send, share_recv, rows_swap_send, rows_swap_recv, rows_send_sem, rows_recv_sem,
 ):
     s, h, b = lax.axis_index("section"), lax.axis_index("head"), lax.axis_index("batch")
     x, z = lax.div(s, 2), lax.div(h, 2)
@@ -80,8 +80,6 @@
         for dx, dy in PLANE[low]:
             at_s, at_h = in_plane(away(dx, x, 1), away(dy, y, 1))
             greet((at_s, at_h, b))
-            if low == 0:
-                greet((at_s, at_h, other))
 
     scalars = [
         pltpu.make_async_copy(slot_order_hbm, slot_order, scalar_sem.at[0]),
@@ -108,7 +106,7 @@
         ).start()
     for copy in whole + fresh:
         copy.start()
-    pl.semaphore_wait(barrier, 29)
+    pl.semaphore_wait(barrier, 22)
 
     def swap(piece):
         low, dz = PIECES[piece]
@@ -142,10 +140,12 @@
 
     def small_pieces(to_s):
         return (
-            (queries.at[:, to_s, :, head_rows], query_all.at[s]),
-            (new_keys.at[:, to_s, :, head_cols], fresh_all.at[0, s]),
-            (new_values.at[:, to_s, :, head_cols], fresh_all.at[1, s]),
+            (queries.at[b, to_s, :, head_rows], query_all.at[b, s]),
+            (new_keys.at[b, to_s, :, head_cols], fresh_all.at[0, b, s]),
+            (new_values.at[b, to_s, :, head_cols], fresh_all.at[1, b, s]),
         )
+
+    small_parts = (query_all, fresh_all.at[0], fresh_all.at[1])
 
     def send_small(step, carry):
         to_s = lax.rem(s + step, 8)
@@ -237,14 +237,17 @@
     ).start()
     pltpu.make_async_copy(values_packed.at[here, 0], values_land.at[0, here_mid], mid_near_recv).start()
 
-    for n, part in enumerate((query_all, fresh_all.at[0], fresh_all.at[1])):
-        wait_for(part, small_recv.at[n])
+    for n, part in enumerate(small_parts):
+        wait_for(part.at[b], small_recv.at[n])
+        remote(part.at[b], part.at[b], share_send.at[n], share_recv.at[n], (s, h, other)).start()
+    for n, part in enumerate(small_parts):
+        wait_for(part.at[other], share_recv.at[n])
     wait_for(key_columns, full_sem.at[0])
     wait_for(value_rows, full_sem.at[1])
 
     def spread_queries(at_s, carry):
         for t in range(2):
-            rows = query_all[at_s, t].astype(F32)
+            rows = query_all[t, at_s].astype(F32)
             for g in range(GROUP):
                 row = (g // 4) * 8 + t * 4 + g % 4
                 for k in range(4):
@@ -277,7 +280,7 @@
             live = jnp.where(lane_prompt == p, lengths[first + p + b * 16], live)
 
         def fresh_row(n, t, slot):
-            rows = fresh_all[n, lax.div(slot, 4), t].astype(F32)
+            rows = fresh_all[n, t, lax.div(slot, 4)].astype(F32)
             return jnp.sum(jnp.where(row4 == lax.rem(slot, 4), rows, 0.0), axis=0, keepdims=True)
 
         questions = jnp.concatenate([query_rows[slot] for slot in slots], axis=0).T
@@ -324,25 +327,36 @@
             )
             for to_b in range(2):
                 cut = slice(to_b * 8, to_b * 8 + 8)
-                rows_send[at_s, to_b, pair] = jnp.concatenate((first[cut], second[cut]), axis=0).astype(BF16)
+                rows_mine[to_b, at_s, pair] = jnp.concatenate((first[cut], second[cut]), axis=0).astype(BF16)
         return carry
 
     lax.fori_loop(0, 8, hand_rows, 0)
 
-    def send_rows(to_s, to_b):
-        remote(
-            rows_send.at[to_s, to_b], rows_land.at[s, b], rows_send_sem, rows_recv_sem, (to_s, h, to_b)
-        ).start()
-
-    def send_rows_step(step, carry):
+    swap_rows = remote(
+        rows_mine.at[other], rows_swap, rows_swap_send, rows_swap_recv, (s, h, other)
+    )
+    swap_rows.start()
+    upper = lax.broadcasted_iota(jnp.int32, (16, HD), 0) < 8
+
+    def merge_rows(at_s, carry):
+        for pair in range(2):
+            first, second = (lax.div(slot_order[at_s * 4 + pair * 2 + n], 16) == b for n in range(2))
+            ours = jnp.where(upper, jnp.where(first, 1.0, 0.0), jnp.where(second, 1.0, 0.0)) > 0.5
+            rows_send[at_s, pair] = jnp.where(
+                ours, rows_mine[b, at_s, pair].astype(F32), rows_swap[at_s, pair].astype(F32)
+            ).astype(BF16)
+        return carry
+
+    swap_rows.wait_recv()
+    lax.fori_loop(0, 8, merge_rows, 0)
+
+    def send_rows(step, carry):
         to_s = lax.rem(s + step, 8)
-        send_rows(to_s, b)
-        send_rows(to_s, other)
-        return carry
-
-    lax.fori_loop(1, 8, send_rows_step, 0)
-    send_rows(s, other)
-    pltpu.make_async_copy(rows_send.at[s, b], rows_land.at[s, b], rows_recv_sem).start()
+        remote(rows_send.at[to_s], rows_land.at[s], rows_send_sem, rows_recv_sem, (to_s, h, b)).start()
+        return carry
+
+    lax.fori_loop(1, 8, send_rows, 0)
+    pltpu.make_async_copy(rows_send.at[s], rows_land.at[s], rows_recv_sem).start()
     owned = [slot_order[s * 4 + k] for k in range(4)]
     lives = [lengths[slot] for slot in owned]
     first_position = (h * 2 + b) * BLOCK
@@ -376,14 +390,11 @@
     turn_keys(0)
     pltpu.make_async_copy(keys_packed.at[here], keys_land.at[here], keys_recv).start()
 
-    owners = [lax.div(slot, 16) for slot in owned]
-
     def assemble(l, carry):
         picked = []
         for k in range(4):
             part = slice((k % 2) * 8, (k % 2) * 8 + 8)
-            first, second = (rows_land[l, n, k // 2].astype(F32)[part] for n in range(2))
-            picked.append(jnp.where(owners[k] == 0, first, second))
+            picked.append(rows_land[l, k // 2].astype(F32)[part])
         for t in range(2):
             attention[t, l] = jnp.concatenate(
                 [
@@ -402,14 +413,15 @@
 
     wait_for(value_rows.at[pl.ds(0, 8)], chip_send)
     wait_for(value_rows.at[pl.ds(0, 14)], line_send)
-    for n, part in enumerate((query_all, fresh_all.at[0], fresh_all.at[1])):
-        wait_for(part.at[pl.ds(0, 7)], small_send.at[n])
+    for n, part in enumerate(small_parts):
+        wait_for(part.at[b, pl.ds(0, 7)], small_send.at[n])
+        wait_for(part.at[b], share_send.at[n])
+    swap_rows.wait_send()
     wait_for(values_packed.at[pl.ds(0, 15), far], mid_send)
     wait_for(values_packed.at[pl.ds(0, 15), 0], mid_near)
     wait_for(keys_packed.at[pl.ds(0, 15)], keys_send)
     wait_for(values_mid, values_send)
     wait_for(rows_send.at[pl.ds(0, 7)], rows_send_sem)
-    wait_for(rows_send.at[0, 0], rows_send_sem)
 
 
 def hand_out(
@@ -464,13 +476,14 @@
             [vmem((32, BLOCK, HD), BF16)] * len(PIECES),
             vmem(plane_shape, BF16), vmem(plane_shape, BF16),
             vmem((3, 16, 4, BLOCK, HD), BF16),
-            vmem((2, 2, 8, 4, KVH * HD), BF16), vmem((8, 2, 4, GROUP * HD), BF16), vmem((32, 16, HD), F32),
-            vmem((2, 8, 2, 4, HD), BF16), vmem((16, 16, HD), F32),
-            vmem((8, 2, 2, 16, HD), BF16), vmem((8, 2, 2, 16, HD), BF16),
+            vmem((2, 2, 8, 4, KVH * HD), BF16), vmem((2, 8, 4, GROUP * HD), BF16), vmem((32, 16, HD), F32),
+            vmem((2, 2, 8, 4, HD), BF16), vmem((16, 16, HD), F32),
+            vmem((2, 8, 2, 16, HD), BF16), vmem((8, 2, 16, HD), BF16),
+            vmem((8, 2, 16, HD), BF16), vmem((8, 2, 16, HD), BF16),
             pltpu.SMEM((32,), jnp.int32), pltpu.SMEM((32,), jnp.int32), pltpu.SMEM((16,), jnp.int32),
             dma((2,)), dma((2,)), dma((2,)), dma, dma((2,)), dma((2,)), dma, dma((len(PIECES),)),
             dma, dma, dma, dma((8,)), dma, dma, dma, dma,
-            dma((3,)), dma((3,)), dma, dma,
+            dma((3,)), dma((3,)), dma((3,)), dma((3,)), dma, dma, dma, dma,
         ],
         compiler_params=pltpu.CompilerParams(
             collective_id=0, has_side_effects=True, vmem_limit_bytes=48 * 2**20

time: 61.5 us -> 61 us (level)
  no operation moved by 1% of the time
where the time goes in v5:
time: 61 us; the launch traced here: 60.9 us
  Pallas kernels  60.2 us (99%)
  between operations  0.64 us (1%)
    pallas_call x1, Pallas kernels, body(): pl.pallas_call(relay, out_shape=tuple((vmem(shape, BF16) for shape in (ro...  57.9 us
    pallas_call x1, Pallas kernels, body(): pl.pallas_call(hand_out, out_shape=tuple((jax.ShapeDtypeStruct(shape, BF1...  2.31 us

profile of v5, /device:TPU:1, one launch (start us, length us, event | category | flops | bytes accessed | tf_op | source)
XLA Modules:
  0.0 60.9 jit_solution(18420163051083784695)
XLA Ops:
  0.6 57.9 %relay.1 = (bf16[2,8,4,512]{3,2,1,0:T(4,128)(2,1)S(1)}, bf16[16,4,4,32,128]{4,3,2,1,0:T(8,128)(2,1)S(1)}, bf16[4,16,4,32,128]{4,3,2,1,0:T(8,128)(2,1)S(1)}, bf16...) custom-call(s32[32]{0:T(128)} %slot_order_hbm.1, ...), custom_call_target="tpu_custom_call" | custom-call | tf_op jit(solution)/shard_map/relay/pallas_call | solution.py:466
  58.6 2.3 %hand_out.1 = (bf16[2,8,4,512]{3,2,1,0:T(4,128)(2,1)}, bf16[8,4,32,1024]{3,2,1,0:T(8,128)(2,1)}, bf16[8,4,32,1024]{3,2,1,0:T(8,128)(2,1)}) custom-call(bf16[2,8,4,512]{3,2,1,0:T(4,128)(2,1)S(1)} %get-tuple-element.9.attention, bf16[16,4,4,32,128]{4,3,2,1,0:T(8,128)(2,1)S(1)} %get-tuple-element.10.keys_land, ...), custom_call_target="tpu_custom_call" | custom-call | tf_op jit(solution)/shard_map/hand_out/pallas_call | solution.py:493

commit v6 on v5

--- a/solution.py
+++ b/solution.py
@@ -126,14 +126,11 @@
             line_send, line_recv.at[low], (s, in_line(to_z), to_b),
         ).start()
 
-    for low in (1, 0):
+    def send_lines(low):
         for dz, to_b in ((1, b), (3, other), (2, b), (1, other), (3, b), (2, other)):
             send_line(low, dz, to_b)
-    for low in (1, 0):
-        remote(
-            keys.at[:, z, owner_low(low), other], keys_near[low].at[mine],
-            line_send, near_recv.at[low], (s, h, other),
-        ).start()
+
+    send_lines(1)
 
     head_rows = pl.ds(pl.multiple_of(h * GROUP * HD, GROUP * HD), GROUP * HD)
     head_cols = pl.ds(pl.multiple_of(h * HD, HD), HD)
@@ -227,11 +224,19 @@
 
     scalars[0].wait()
     scalars[1].wait()
+    for piece in range(2):
+        take_values(piece)
+    send_lines(0)
     lax.fori_loop(1, 8, send_small, 0)
     for n, (src, dst) in enumerate(small_pieces(s)):
         pltpu.make_async_copy(src, dst, small_recv.at[n]).start()
-    for piece in range(len(PIECES)):
+    for piece in range(2, len(PIECES)):
         take_values(piece)
+    for low in (1, 0):
+        remote(
+            keys.at[:, z, owner_low(low), other], keys_near[low].at[mine],
+            line_send, near_recv.at[low], (s, h, other),
+        ).start()
     pltpu.make_async_copy(
         values_packed.at[here, far], values_mid.at[:, here_mid], mid_recv.at[group_of(0, 0)]
     ).start()

time: 61 us -> 61.8 us (1.013)
  Pallas kernels: 60.2 us -> 61.1 us
    pallas_call x1, Pallas kernels: 57.9 us -> 58.8 us  [body(): pl.pallas_call(relay, out_shape=tuple((vmem(shape, BF16) for shape in (ro...]
where the time goes in v6:
time: 61.8 us; the launch traced here: 61.7 us
  Pallas kernels  61.1 us (99%)
  between operations  0.64 us (1%)
    pallas_call x1, Pallas kernels, body(): pl.pallas_call(relay, out_shape=tuple((vmem(shape, BF16) for shape in (ro...  58.8 us
    pallas_call x1, Pallas kernels, body(): pl.pallas_call(hand_out, out_shape=tuple((jax.ShapeDtypeStruct(shape, BF1...  2.31 us

profile of v6, /device:TPU:1, one launch (start us, length us, event | category | flops | bytes accessed | tf_op | source)
XLA Modules:
  0.0 61.7 jit_solution(853170459724137057)
XLA Ops:
  0.6 58.8 %relay.1 = (bf16[2,8,4,512]{3,2,1,0:T(4,128)(2,1)S(1)}, bf16[16,4,4,32,128]{4,3,2,1,0:T(8,128)(2,1)S(1)}, bf16[4,16,4,32,128]{4,3,2,1,0:T(8,128)(2,1)S(1)}, bf16...) custom-call(s32[32]{0:T(128)} %slot_order_hbm.1, ...), custom_call_target="tpu_custom_call" | custom-call | tf_op jit(solution)/shard_map/relay/pallas_call | solution.py:471
  59.4 2.3 %hand_out.1 = (bf16[2,8,4,512]{3,2,1,0:T(4,128)(2,1)}, bf16[8,4,32,1024]{3,2,1,0:T(8,128)(2,1)}, bf16[8,4,32,1024]{3,2,1,0:T(8,128)(2,1)}) custom-call(bf16[2,8,4,512]{3,2,1,0:T(4,128)(2,1)S(1)} %get-tuple-element.9.attention, bf16[16,4,4,32,128]{4,3,2,1,0:T(8,128)(2,1)S(1)} %get-tuple-element.10.keys_land, ...), custom_call_target="tpu_custom_call" | custom-call | tf_op jit(solution)/shard_map/hand_out/pallas_call | solution.py:498

commit v7 on v5

--- a/solution.py
+++ b/solution.py
@@ -19,10 +19,6 @@
     0: ((1, 0), (0, 2), (3, 2), (1, 2), (3, 0), (2, 2), (2, 0)),
 }
 PIECES = ((1, 1), (1, 3), (1, 2), (0, 1), (0, 3), (0, 2), (1, 0), (0, 0))
-
-
-def group_of(dx, low):
-    return low * 4 + dx
 
 
 def relay(
@@ -43,7 +39,7 @@
     sign = 1 - 2 * b
     mine = pl.ds(b * 16, 16)
     here = x * 4 + y
-    here_mid = x * 4 + y_low * 2 + lax.div(y, 2)
+    here_mid = (x, y_low, lax.div(y, 2))
 
     def remote(src, dst, send_sem, recv_sem, to):
         return pltpu.make_async_remote_copy(
@@ -180,20 +176,24 @@
         if dz:
             for dx, dy in PLANE[low]:
                 send_plane(
-                    lambda to: values_packed.at[to, at_z], dx, dy, values_mid.at[at_z - 1, here_mid],
-                    mid_send, mid_recv.at[group_of(dx, low)],
+                    lambda to: values_packed.at[to, at_z], dx, dy, values_mid.at[at_z - 1, *here_mid],
+                    mid_send, mid_recv.at[piece],
                 )
+            if low == 0:
+                pltpu.make_async_copy(
+                    values_packed.at[here, at_z], values_mid.at[at_z - 1, *here_mid], mid_recv.at[piece]
+                ).start()
 
     far = pl.ds(1, 3)
 
-    def forward_values(dx, low):
-        group = group_of(dx, low)
-        wait_for(values_mid.at[:, pl.ds(0, 2)], mid_recv.at[group])
-        pair = pl.ds(away(dx, x, -sign) * 4 + owner_low(low) * 2, 2)
-        for dz in (1, 3, 2):
+    def forward_values(piece):
+        low, dz = PIECES[piece]
+        at_z = away(dz, 0, sign)
+        wait_for(values_mid.at[0, :, 0], mid_recv.at[piece])
+        for at_x in range(4):
             remote(
-                values_mid.at[dz - 1, pair], values_land.at[dz, pair],
-                values_send, values_recv, (s, in_line(away(dz, z, 1)), b),
+                values_mid.at[at_z - 1, at_x, owner_low(low)], values_land.at[at_z, at_x, owner_low(low)],
+                values_send, values_recv, (s, in_line(away(dz, z, sign)), b),
             ).start()
 
     def take_near_keys(low):
@@ -207,7 +207,7 @@
     def send_near_values():
         for dx, dy in PLANE[1] + PLANE[0]:
             send_plane(
-                lambda to: values_packed.at[to, 0], dx, dy, values_land.at[0, here_mid], mid_near, mid_near_recv
+                lambda to: values_packed.at[to, 0], dx, dy, values_land.at[0, *here_mid], mid_near, mid_near_recv
             )
 
     def send_near_keys():
@@ -232,10 +232,7 @@
         pltpu.make_async_copy(src, dst, small_recv.at[n]).start()
     for piece in range(len(PIECES)):
         take_values(piece)
-    pltpu.make_async_copy(
-        values_packed.at[here, far], values_mid.at[:, here_mid], mid_recv.at[group_of(0, 0)]
-    ).start()
-    pltpu.make_async_copy(values_packed.at[here, 0], values_land.at[0, here_mid], mid_near_recv).start()
+    pltpu.make_async_copy(values_packed.at[here, 0], values_land.at[0, *here_mid], mid_near_recv).start()
 
     for n, part in enumerate(small_parts):
         wait_for(part.at[b], small_recv.at[n])
@@ -380,11 +377,11 @@
     lax.fori_loop(0, 8, place_fresh, 0)
     take_near_keys(1)
     take_near_keys(0)
-    for dx in (1, 3, 2, 0):
-        forward_values(dx, 1)
+    for piece in range(3):
+        forward_values(piece)
     send_near_values()
-    for dx in (1, 3, 2, 0):
-        forward_values(dx, 0)
+    for piece in range(3, 6):
+        forward_values(piece)
     send_near_keys()
     turn_keys(1)
     turn_keys(0)
@@ -440,7 +437,7 @@
             for k in range(4):
                 landed = keys_land[x * 4 + y_high * 2 + y_low, lax.rem(from_z - z + 4, 4), k]
                 keys[l, k, :, cut] = jnp.where(kept[k], landed, keys_fresh[l, k, :, cut])
-                landed = values_land[lax.rem(z - from_z + 4, 4), x * 4 + y_low * 2 + y_high, k]
+                landed = values_land[lax.rem(z - from_z + 4, 4), x, y_low, y_high, k]
                 values[l, k, :, cut] = jnp.where(kept[k], landed, values_fresh[l, k, :, cut])
         for n, (src, dst) in enumerate(((keys, keys_out), (values, values_out))):
             copies.append(pltpu.make_async_copy(src.at[l], dst.at[l], sem.at[n * 8 + l]))
@@ -458,7 +455,7 @@
     vmem_spec = pl.BlockSpec(memory_space=pltpu.VMEM)
     dma, vmem = pltpu.SemaphoreType.DMA, pltpu.VMEM
     rows_shape, cache_shape = (2, 8, 4, 4 * HD), (8, 4, BLOCK, KVH * HD)
-    plane_shape, line_shape = (16, 4, 4, BLOCK, HD), (4, 16, 4, BLOCK, HD)
+    plane_shape, line_shape = (16, 4, 4, BLOCK, HD), (4, 4, 2, 2, 4, BLOCK, HD)
 
     def in_hbm(array):
         return pltpu.with_memory_space_constraint(array, pltpu.HBM)
@@ -475,14 +472,14 @@
             [vmem((3, 32, BLOCK, HD), BF16)] * 2, [vmem((32, BLOCK, HD), BF16)] * 2,
             [vmem((32, BLOCK, HD), BF16)] * len(PIECES),
             vmem(plane_shape, BF16), vmem(plane_shape, BF16),
-            vmem((3, 16, 4, BLOCK, HD), BF16),
+            vmem((3, *line_shape[1:]), BF16),
             vmem((2, 2, 8, 4, KVH * HD), BF16), vmem((2, 8, 4, GROUP * HD), BF16), vmem((32, 16, HD), F32),
             vmem((2, 2, 8, 4, HD), BF16), vmem((16, 16, HD), F32),
             vmem((2, 8, 2, 16, HD), BF16), vmem((8, 2, 16, HD), BF16),
             vmem((8, 2, 16, HD), BF16), vmem((8, 2, 16, HD), BF16),
             pltpu.SMEM((32,), jnp.int32), pltpu.SMEM((32,), jnp.int32), pltpu.SMEM((16,), jnp.int32),
             dma((2,)), dma((2,)), dma((2,)), dma, dma((2,)), dma((2,)), dma, dma((len(PIECES),)),
-            dma, dma, dma, dma((8,)), dma, dma, dma, dma,
+            dma, dma, dma, dma((6,)), dma, dma, dma, dma,
             dma((3,)), dma((3,)), dma((3,)), dma((3,)), dma, dma, dma, dma,
         ],
         compiler_params=pltpu.CompilerParams(

time: 61 us -> 61 us (level)
  no operation moved by 1% of the time
where the time goes in v7:
time: 61 us; the launch traced here: 60.9 us
  Pallas kernels  60.2 us (99%)
  between operations  0.64 us (1%)
    pallas_call x1, Pallas kernels, body(): pl.pallas_call(relay, out_shape=tuple((vmem(shape, BF16) for shape in (ro...  57.9 us
    pallas_call x1, Pallas kernels, body(): pl.pallas_call(hand_out, out_shape=tuple((jax.ShapeDtypeStruct(shape, BF1...  2.31 us

profile of v7, /device:TPU:1, one launch (start us, length us, event | category | flops | bytes accessed | tf_op | source)
XLA Modules:
  0.0 60.9 jit_solution(1100885124577949283)
XLA Ops:
  0.6 57.9 %relay.1 = (bf16[2,8,4,512]{3,2,1,0:T(4,128)(2,1)S(1)}, bf16[16,4,4,32,128]{4,3,2,1,0:T(8,128)(2,1)S(1)}, bf16[4,4,2,2,4,32,128]{6,5,4,3,2,1,0:T(8,128)(2,1)S(1)...) custom-call(s32[32]{0:T(128)} %slot_order_hbm.1, ...), custom_call_target="tpu_custom_call" | custom-call | tf_op jit(solution)/shard_map/relay/pallas_call | solution.py:463
  58.5 2.3 %hand_out.1 = (bf16[2,8,4,512]{3,2,1,0:T(4,128)(2,1)}, bf16[8,4,32,1024]{3,2,1,0:T(8,128)(2,1)}, bf16[8,4,32,1024]{3,2,1,0:T(8,128)(2,1)}) custom-call(bf16[2,8,4,512]{3,2,1,0:T(4,128)(2,1)S(1)} %get-tuple-element.9.attention, bf16[16,4,4,32,128]{4,3,2,1,0:T(8,128)(2,1)S(1)} %get-tuple-element.10.keys_land, ...), custom_call_target="tpu_custom_call" | custom-call | tf_op jit(solution)/shard_map/hand_out/pallas_call | solution.py:490

commit v8 on v7

--- a/solution.py
+++ b/solution.py
@@ -92,16 +92,14 @@
     ]
     for copy in scalars:
         copy.start()
-    for piece, (low, dz) in enumerate(PIECES):
+    def own_piece(piece):
+        low, dz = PIECES[piece]
         pltpu.make_async_copy(
             values.at[:, away(dz, z, sign), owner_low(low), b], values_chip[piece].at[mine], chip_recv.at[piece]
         ).start()
-    for low in (1, 0):
-        pltpu.make_async_copy(
-            keys.at[:, z, owner_low(low), b], keys_near[low].at[mine], near_recv.at[low]
-        ).start()
-    for copy in whole + fresh:
-        copy.start()
+
+    own_piece(0)
+    own_piece(1)
     pl.semaphore_wait(barrier, 22)
 
     def swap(piece):
@@ -130,6 +128,9 @@
             keys.at[:, z, owner_low(low), other], keys_near[low].at[mine],
             line_send, near_recv.at[low], (s, h, other),
         ).start()
+
+    for piece in range(2, len(PIECES)):
+        own_piece(piece)
 
     head_rows = pl.ds(pl.multiple_of(h * GROUP * HD, GROUP * HD), GROUP * HD)
     head_cols = pl.ds(pl.multiple_of(h * HD, HD), HD)
@@ -230,7 +231,15 @@
     lax.fori_loop(1, 8, send_small, 0)
     for n, (src, dst) in enumerate(small_pieces(s)):
         pltpu.make_async_copy(src, dst, small_recv.at[n]).start()
-    for piece in range(len(PIECES)):
+    for piece in range(2):
+        take_values(piece)
+    for low in (1, 0):
+        pltpu.make_async_copy(
+            keys.at[:, z, owner_low(low), b], keys_near[low].at[mine], near_recv.at[low]
+        ).start()
+    for copy in whole + fresh:
+        copy.start()
+    for piece in range(2, len(PIECES)):
         take_values(piece)
     pltpu.make_async_copy(values_packed.at[here, 0], values_land.at[0, *here_mid], mid_near_recv).start()
 

time: 61 us -> 61 us (level)
  no operation moved by 1% of the time
where the time goes in v8:
time: 61 us; the launch traced here: 60.9 us
  Pallas kernels  60.2 us (99%)
  between operations  0.64 us (1%)
    pallas_call x1, Pallas kernels, body(): pl.pallas_call(relay, out_shape=tuple((vmem(shape, BF16) for shape in (ro...  57.9 us
    pallas_call x1, Pallas kernels, body(): pl.pallas_call(hand_out, out_shape=tuple((jax.ShapeDtypeStruct(shape, BF1...  2.31 us

profile of v8, /device:TPU:1, one launch (start us, length us, event | category | flops | bytes accessed | tf_op | source)
XLA Modules:
  0.0 60.9 jit_solution(14889537077565243769)
XLA Ops:
  0.6 57.9 %relay.1 = (bf16[2,8,4,512]{3,2,1,0:T(4,128)(2,1)S(1)}, bf16[16,4,4,32,128]{4,3,2,1,0:T(8,128)(2,1)S(1)}, bf16[4,4,2,2,4,32,128]{6,5,4,3,2,1,0:T(8,128)(2,1)S(1)...) custom-call(s32[32]{0:T(128)} %slot_order_hbm.1, ...), custom_call_target="tpu_custom_call" | custom-call | tf_op jit(solution)/shard_map/relay/pallas_call | solution.py:472
  58.6 2.3 %hand_out.1 = (bf16[2,8,4,512]{3,2,1,0:T(4,128)(2,1)}, bf16[8,4,32,1024]{3,2,1,0:T(8,128)(2,1)}, bf16[8,4,32,1024]{3,2,1,0:T(8,128)(2,1)}) custom-call(bf16[2,8,4,512]{3,2,1,0:T(4,128)(2,1)S(1)} %get-tuple-element.9.attention, bf16[16,4,4,32,128]{4,3,2,1,0:T(8,128)(2,1)S(1)} %get-tuple-element.10.keys_land, ...), custom_call_target="tpu_custom_call" | custom-call | tf_op jit(solution)/shard_map/hand_out/pallas_call | solution.py:499
